TPU v7x, 32 devices: a whole 2x2x4 slice. The times are simulated.
32 devices in a mesh: fsdp: 4 (over y, x), dp: 8 (over z, core).
Axes of the slice: x: 2, y: 2, z: 4, core: 2. Of those that a mesh axis runs over, the one named last changes fastest.
Arguments:
- tokens: bfloat16 [16384, 960], P(('fsdp', 'dp')), may hold values from -6 to 6
- span_table: int32 [8, 8], P('dp'), may hold values from 0 to 7, as said below
- w_query: bfloat16 [960, 960], P('fsdp'), may hold values from -0.1875 to 0.1875
- w_key: bfloat16 [960, 320], P('fsdp'), may hold values from -0.1875 to 0.1875
- w_value: bfloat16 [960, 320], P('fsdp'), may hold values from -0.1875 to 0.1875
- w_out: bfloat16 [960, 960], P('fsdp'), may hold values from -3.5 to 3.5
- w_gate: bfloat16 [960, 2560], P('fsdp'), may hold values from -0.1875 to 0.1875
- w_up: bfloat16 [960, 2560], P('fsdp'), may hold values from -0.1875 to 0.1875
- w_down: bfloat16 [2560, 960], P('fsdp'), may hold values from -0.125 to 0.125
- gain_attn: bfloat16 [960], P('fsdp'), may hold values from 0.099609375 to 1.8984375
- gain_ffn: bfloat16 [960], P('fsdp'), may hold values from 0.099609375 to 1.8984375
- cotangent: bfloat16 [16384, 960], P(('fsdp', 'dp')), may hold values from -6 to 6
Outputs:
- output: bfloat16 [16384, 960], P(('fsdp', 'dp'))
- grad_tokens: float32 [16384, 960], P(('fsdp', 'dp'))
- grad_w_query: float32 [960, 960], P('fsdp')
- grad_w_key: float32 [960, 320], P('fsdp')
- grad_w_value: float32 [960, 320], P('fsdp')
- grad_w_out: float32 [960, 960], P('fsdp')
- grad_w_gate: float32 [960, 2560], P('fsdp')
- grad_w_up: float32 [960, 2560], P('fsdp')
- grad_w_down: float32 [2560, 960], P('fsdp')
- grad_gain_attn: float32 [960], P('fsdp')
- grad_gain_ffn: float32 [960], P('fsdp')
Inputs may be any that keep to these rules, and one draw needn't show every extreme that they name: `span_table`: each row is a permutation of the 8 blocks of a sequence over the slots.
All inputs are finite; a program needn't handle non-finite values.
Results may differ from a plain program's by a relative error of at most 0.022.
Values may be sent and summed in bfloat16 or wider, within the bound.
A program may use at most 192 MiB of HBM per device.

v0:
```python
import jax
import jax.numpy as jnp
from jax import lax
from jax.sharding import PartitionSpec as P

HEADS = 15
KV_HEADS = 5
HEAD_DIM = 64
epsilon = 1e-05
rope_base = 100000.0


def rope_tables(places, head_dim):
    half_dim = head_dim // 2
    rates = rope_base ** (-2.0 * jnp.arange(half_dim, dtype=jnp.float32) / head_dim)
    angles = places.astype(jnp.float32)[:, None] * rates[None, :]
    return (jnp.cos(angles)[:, None, :], jnp.sin(angles)[:, None, :])


def rotate(field, cosine, sine_part):
    half_dim = field.shape[-1] // 2
    first = field[..., :half_dim]
    second = field[..., half_dim:]
    return jnp.concatenate(
        [first * cosine - second * sine_part, second * cosine + first * sine_part], axis=-1
    )


def rms_scale(values):
    return lax.rsqrt(jnp.mean(values * values, axis=-1, keepdims=True) + epsilon)


def norm_back(grad_normed, values, scale_rows, gain):
    scaled = values * scale_rows
    weighted = grad_normed * gain
    grad_values = scale_rows * (
        weighted - scaled * jnp.mean(weighted * scaled, axis=-1, keepdims=True)
    )
    return (grad_values, jnp.sum(grad_normed * scaled, axis=0))


def matmul(left, right):
    return jnp.dot(left, right, preferred_element_type=jnp.float32)


def outer(left, right):
    return jnp.einsum("rd,re->de", left, right, preferred_element_type=jnp.float32)


def inner_back(grad_rows, weight):
    return jnp.einsum("re,de->rd", grad_rows, weight, preferred_element_type=jnp.float32)


def keys_by_head(gathered, groups, seqs):
    spread = gathered.reshape(groups, seqs, -1, KV_HEADS, HEAD_DIM)
    return spread.transpose(3, 1, 0, 2, 4).reshape(KV_HEADS, seqs, -1, HEAD_DIM)


def on_device(
    tokens,
    span_table,
    w_query,
    w_key,
    w_value,
    w_out,
    w_gate,
    w_up,
    w_down,
    gain_attn,
    gain_ffn,
    cotangent,
):
    groups = lax.axis_size("fsdp")
    index = lax.axis_index("fsdp")
    rows = tokens.shape[0]
    seqs = span_table.shape[0]
    span = rows // (2 * seqs)
    per_kv = HEADS // KV_HEADS
    scale = HEAD_DIM ** (-0.5)
    full = (
        lax.all_gather(w_query, "fsdp", axis=0, tiled=True),
        lax.all_gather(w_key, "fsdp", axis=0, tiled=True),
        lax.all_gather(w_value, "fsdp", axis=0, tiled=True),
        lax.all_gather(w_out, "fsdp", axis=0, tiled=True),
        lax.all_gather(w_gate, "fsdp", axis=0, tiled=True),
        lax.all_gather(w_up, "fsdp", axis=0, tiled=True),
        lax.all_gather(w_down, "fsdp", axis=0, tiled=True),
        lax.all_gather(gain_attn, "fsdp", axis=0, tiled=True),
        lax.all_gather(gain_ffn, "fsdp", axis=0, tiled=True),
    )
    (
        query_full,
        key_full,
        value_full,
        out_full,
        gate_full,
        up_full,
        down_full,
        attn_gain,
        ffn_gain,
    ) = full
    attn_gain = attn_gain.astype(jnp.float32)
    ffn_gain = ffn_gain.astype(jnp.float32)
    offsets = jnp.arange(span, dtype=jnp.int32)
    mine = lax.dynamic_slice_in_dim(span_table, 2 * index, 2, 1)
    query_place = (mine[:, :, None] * span + offsets).reshape(seqs, 2 * span)
    key_place = (span_table.reshape(seqs, groups, 2)[:, :, :, None] * span + offsets).reshape(
        seqs, -1
    )
    allowed = query_place[:, None, :, None] >= key_place[:, None, None, :]
    cosine, sine_part = rope_tables(query_place.reshape(-1), HEAD_DIM)
    inputs = tokens.astype(jnp.float32)
    scale_one = rms_scale(inputs)
    normed_one = (inputs * scale_one * attn_gain).astype(jnp.bfloat16)
    query_rows = rotate(
        matmul(normed_one, query_full).reshape(rows, HEADS, HEAD_DIM), cosine, sine_part
    ).astype(jnp.bfloat16)
    key_rows = (
        rotate(matmul(normed_one, key_full).reshape(rows, KV_HEADS, HEAD_DIM), cosine, sine_part)
        .astype(jnp.bfloat16)
        .reshape(rows, -1)
    )
    value_rows = matmul(normed_one, value_full).astype(jnp.bfloat16)
    key_all, value_all = (
        lax.all_gather(key_rows, "fsdp", axis=0, tiled=True),
        lax.all_gather(value_rows, "fsdp", axis=0, tiled=True),
    )
    key_heads = keys_by_head(key_all, groups, seqs)
    value_heads = keys_by_head(value_all, groups, seqs)
    query_heads = query_rows.reshape(seqs, 2 * span, KV_HEADS, per_kv, HEAD_DIM).transpose(
        2, 0, 3, 1, 4
    )

    def forward_head(operands):
        query, keys, values = operands
        raw_scores = (
            jnp.einsum("sgqd,skd->sgqk", query, keys, preferred_element_type=jnp.float32) * scale
        )
        scores = jnp.where(allowed, raw_scores, -1e30)
        row_max = jnp.max(scores, axis=-1, keepdims=True)
        powers = jnp.exp(scores - row_max)
        totals = jnp.sum(powers, axis=-1, keepdims=True)
        weights = (powers / totals).astype(jnp.bfloat16)
        mixed = jnp.einsum("sgqk,skd->sgqd", weights, values, preferred_element_type=jnp.float32)
        return (mixed, row_max + jnp.log(totals))

    mixed_heads, log_sums = lax.map(forward_head, (query_heads, key_heads, value_heads))
    attended = (
        mixed_heads.transpose(1, 3, 0, 2, 4).reshape(rows, HEADS * HEAD_DIM).astype(jnp.bfloat16)
    )
    hidden = inputs + matmul(attended, out_full)
    scale_two = rms_scale(hidden)
    normed_two = (hidden * scale_two * ffn_gain).astype(jnp.bfloat16)
    gate = matmul(normed_two, gate_full)
    upward = matmul(normed_two, up_full)
    sigma = jax.nn.sigmoid(gate)
    activated = gate * sigma
    inner = (activated * upward).astype(jnp.bfloat16)
    output = (hidden + matmul(inner, down_full)).astype(jnp.bfloat16)
    back = (
        lax.all_gather(w_query, "fsdp", axis=0, tiled=True),
        lax.all_gather(w_key, "fsdp", axis=0, tiled=True),
        lax.all_gather(w_value, "fsdp", axis=0, tiled=True),
        lax.all_gather(w_out, "fsdp", axis=0, tiled=True),
        lax.all_gather(w_gate, "fsdp", axis=0, tiled=True),
        lax.all_gather(w_up, "fsdp", axis=0, tiled=True),
        lax.all_gather(w_down, "fsdp", axis=0, tiled=True),
        lax.all_gather(gain_attn, "fsdp", axis=0, tiled=True),
        lax.all_gather(gain_ffn, "fsdp", axis=0, tiled=True),
    )
    query_back, key_back, value_back, out_back, gate_back, up_back, down_back = back[:7]
    grad_out = cotangent.astype(jnp.float32)
    grad_w_down = outer(inner, cotangent)
    grad_inner = inner_back(cotangent, down_back)
    grad_gate = (grad_inner * upward * sigma * (1.0 + gate * (1.0 - sigma))).astype(jnp.bfloat16)
    grad_up = (grad_inner * activated).astype(jnp.bfloat16)
    grad_w_gate = outer(normed_two, grad_gate)
    grad_w_up = outer(normed_two, grad_up)
    grad_normed_two = inner_back(grad_gate, gate_back) + inner_back(grad_up, up_back)
    grad_hidden_norm, grad_gain_ffn = norm_back(grad_normed_two, hidden, scale_two, ffn_gain)
    grad_hidden = grad_out + grad_hidden_norm
    grad_branch = grad_hidden.astype(jnp.bfloat16)
    grad_w_out = outer(attended, grad_branch)
    grad_attended = inner_back(grad_branch, out_back).astype(jnp.bfloat16)
    grad_heads = grad_attended.reshape(seqs, 2 * span, KV_HEADS, per_kv, HEAD_DIM).transpose(
        2, 0, 3, 1, 4
    )

    def backward_head(operands):
        query, keys, values, grad_mixed, log_sum = operands
        raw_scores = (
            jnp.einsum("sgqd,skd->sgqk", query, keys, preferred_element_type=jnp.float32) * scale
        )
        scores = jnp.where(allowed, raw_scores, -1e30)
        probs = jnp.exp(scores - log_sum)
        weights = probs.astype(jnp.bfloat16)
        grad_values = jnp.einsum(
            "sgqk,sgqd->skd", weights, grad_mixed, preferred_element_type=jnp.float32
        )
        grad_probs = jnp.einsum(
            "sgqd,skd->sgqk", grad_mixed, values, preferred_element_type=jnp.float32
        )
        centred = jnp.sum(probs * grad_probs, axis=-1, keepdims=True)
        grad_scores = (probs * (grad_probs - centred) * scale).astype(jnp.bfloat16)
        grad_query = jnp.einsum(
            "sgqk,skd->sgqd", grad_scores, keys, preferred_element_type=jnp.float32
        )
        grad_keys = jnp.einsum(
            "sgqk,sgqd->skd", grad_scores, query, preferred_element_type=jnp.float32
        )
        return (grad_query, grad_keys, grad_values)

    grad_query_heads, grad_key_heads, grad_value_heads = lax.map(
        backward_head, (query_heads, key_heads, value_heads, grad_heads, log_sums)
    )

    def to_gathered(field):
        spread = field.reshape(KV_HEADS, seqs, groups, 2 * span, HEAD_DIM)
        return spread.transpose(2, 1, 3, 0, 4).reshape(groups * rows, KV_HEADS * HEAD_DIM)

    grad_key_turned, grad_value_sum = (
        lax.psum_scatter(
            to_gathered(grad_key_heads).astype(jnp.bfloat16),
            "fsdp",
            scatter_dimension=0,
            tiled=True,
        ).astype(jnp.float32),
        lax.psum_scatter(
            to_gathered(grad_value_heads).astype(jnp.bfloat16),
            "fsdp",
            scatter_dimension=0,
            tiled=True,
        ).astype(jnp.float32),
    )
    grad_key_rows = (
        rotate(grad_key_turned.reshape(rows, KV_HEADS, HEAD_DIM), cosine, -sine_part)
        .reshape(rows, -1)
        .astype(jnp.bfloat16)
    )
    grad_query_turned = grad_query_heads.transpose(1, 3, 0, 2, 4).reshape(rows, HEADS, HEAD_DIM)
    grad_query_rows = (
        rotate(grad_query_turned, cosine, -sine_part).reshape(rows, -1).astype(jnp.bfloat16)
    )
    grad_value_rows = grad_value_sum.astype(jnp.bfloat16)
    grad_w_query = outer(normed_one, grad_query_rows)
    grad_w_key = outer(normed_one, grad_key_rows)
    grad_w_value = outer(normed_one, grad_value_rows)
    grad_normed_one = (
        inner_back(grad_query_rows, query_back)
        + inner_back(grad_key_rows, key_back)
        + inner_back(grad_value_rows, value_back)
    )
    grad_input_norm, grad_gain_attn = norm_back(grad_normed_one, inputs, scale_one, attn_gain)
    grad_tokens = grad_hidden + grad_input_norm
    owned = (
        lax.psum_scatter(
            grad_w_query.astype(jnp.bfloat16), "fsdp", scatter_dimension=0, tiled=True
        ).astype(jnp.float32),
        lax.psum_scatter(
            grad_w_key.astype(jnp.bfloat16), "fsdp", scatter_dimension=0, tiled=True
        ).astype(jnp.float32),
        lax.psum_scatter(
            grad_w_value.astype(jnp.bfloat16), "fsdp", scatter_dimension=0, tiled=True
        ).astype(jnp.float32),
        lax.psum_scatter(
            grad_w_out.astype(jnp.bfloat16), "fsdp", scatter_dimension=0, tiled=True
        ).astype(jnp.float32),
        lax.psum_scatter(
            grad_w_gate.astype(jnp.bfloat16), "fsdp", scatter_dimension=0, tiled=True
        ).astype(jnp.float32),
        lax.psum_scatter(
            grad_w_up.astype(jnp.bfloat16), "fsdp", scatter_dimension=0, tiled=True
        ).astype(jnp.float32),
        lax.psum_scatter(
            grad_w_down.astype(jnp.bfloat16), "fsdp", scatter_dimension=0, tiled=True
        ).astype(jnp.float32),
        lax.psum_scatter(
            grad_gain_attn.astype(jnp.bfloat16), "fsdp", scatter_dimension=0, tiled=True
        ).astype(jnp.float32),
        lax.psum_scatter(
            grad_gain_ffn.astype(jnp.bfloat16), "fsdp", scatter_dimension=0, tiled=True
        ).astype(jnp.float32),
    )
    summed = (
        lax.psum(owned[0].astype(jnp.bfloat16), "dp").astype(jnp.float32),
        lax.psum(owned[1].astype(jnp.bfloat16), "dp").astype(jnp.float32),
        lax.psum(owned[2].astype(jnp.bfloat16), "dp").astype(jnp.float32),
        lax.psum(owned[3].astype(jnp.bfloat16), "dp").astype(jnp.float32),
        lax.psum(owned[4].astype(jnp.bfloat16), "dp").astype(jnp.float32),
        lax.psum(owned[5].astype(jnp.bfloat16), "dp").astype(jnp.float32),
        lax.psum(owned[6].astype(jnp.bfloat16), "dp").astype(jnp.float32),
        lax.psum(owned[7].astype(jnp.bfloat16), "dp").astype(jnp.float32),
        lax.psum(owned[8].astype(jnp.bfloat16), "dp").astype(jnp.float32),
    )
    return (
        output,
        grad_tokens,
        summed[0],
        summed[1],
        summed[2],
        summed[3],
        summed[4],
        summed[5],
        summed[6],
        summed[7],
        summed[8],
    )


def solution(mesh):
    return jax.shard_map(
        on_device,
        mesh=mesh,
        in_specs=(
            P(("fsdp", "dp"), None),
            P("dp", None),
            P("fsdp", None),
            P("fsdp", None),
            P("fsdp", None),
            P("fsdp", None),
            P("fsdp", None),
            P("fsdp", None),
            P("fsdp", None),
            P("fsdp"),
            P("fsdp"),
            P(("fsdp", "dp"), None),
        ),
        out_specs=(
            P(("fsdp", "dp"), None),
            P(("fsdp", "dp"), None),
            P("fsdp", None),
            P("fsdp", None),
            P("fsdp", None),
            P("fsdp", None),
            P("fsdp", None),
            P("fsdp", None),
            P("fsdp", None),
            P("fsdp"),
            P("fsdp"),
        ),
        check_vma=False,
    )
```

profile of v0, /device:TPU:0, one launch (start us, length us, event | category | flops | bytes accessed | tf_op | source)
XLA Modules:
  0.0 1192.5 jit_solution(17150730521787951973)
XLA Ops:
  12.5 11.3 all-reduce.9
  23.9 10.8 all-gather
  38.3 10.2 all-gather.1
  55.7 11.7 all-gather.12.cloned.1.call-done
  74.5 23.9 %all-gather.14.cloned.1.call-done = bf16[2048,320]{0,1:T(8,128)(2,1)} async-done(((bf16[512,320]{0,1:T(8,128)(2,1)}), bf16[2048,320]{0,1:T(8,128)(2,1)}) %all-gather.14.cloned.1.call-update) | async-done | bytes 1310736 | tf_op jit(solution)/shard_map/all_gather | solution.py:126
  106.5 28.1 %all-gather.10.cloned.1.call-done = bf16[960,960]{1,0:T(8,128)(2,1)} async-done(((bf16[240,960]{1,0:T(8,128)(2,1)}), bf16[960,960]{1,0:T(8,128)(2,1)}) %all-gather.10.cloned.1.call-update) | async-done | bytes 1843216 | tf_op jit(solution)/shard_map/all_gather | solution.py:81
  137.9 104.2 %while.30 = (s32[]{:T(128)}, bf16[5,1,3,512,64]{3,4,2,1,0:T(8,128)(2,1)}, f32[5,1,3,512,1]{3,2,4,1,0:T(4,128)S(1)}, bf16[5,1,3,512,64]{3,4,2,1,0:T(8,128)(2,1)S(...) while((s32[]{:T(128)}, ...), condition=%wide.region_4.5_spmd.clone.clone, body=%wide.region_1.4_spmd.clone.sunk.clone | while | flops 844102144 | bytes 43124832 | solution.py:147
  151.4 7.4 fusion.206
  165.4 6.8 fusion.205
  172.2 7.4 fusion.206
  186.1 6.8 fusion.205
  192.9 7.4 fusion.206
  213.6 7.4 fusion.206
  234.3 7.4 fusion.206
  246.9 7.8 fusion.127
  254.7 36.7 %all-gather.18.cloned.1.call-done = bf16[960,2560]{1,0:T(8,128)(2,1)} async-done(((bf16[240,2560]{1,0:T(8,128)(2,1)}), bf16[960,2560]{1,0:T(8,128)(2,1)}) %all-gather.18.cloned.1.call-update) | async-done | bytes 4915216 | tf_op jit(solution)/shard_map/all_gather | solution.py:85
  291.4 7.0 fusion.126
  298.5 53.5 %all-gather.22.cloned.1.call-done = bf16[2560,960]{0,1:T(8,128)(2,1)} async-done(((bf16[640,960]{0,1:T(8,128)(2,1)}), bf16[2560,960]{0,1:T(8,128)(2,1)}) %all-gather.22.cloned.1.call-update) | async-done | bytes 4915216 | tf_op jit(solution)/shard_map/all_gather | solution.py:87
  352.0 10.4 multiply_convert_fusion.1
  375.3 290.0 %while.31 = (s32[]{:T(128)}, f32[5,1,3,512,64]{3,4,2,1,0:T(8,128)S(1)}, bf16[5,1,2048,64]{2,3,1,0:T(8,128)(2,1)}, bf16[5,1,2048,64]{2,3,1,0:T(8,128)(2,1)}, bf16...) while((s32[]{:T(128)}, ...), condition=%wide.region_9.10_spmd.clone.clone, body=%wide.region_7.9_spmd.clone.sunk.clone | while | flops 2096110592 | bytes 198116496 | solution.py:213
  384.6 7.4 fusion.217
  392.0 21.3 %fusion.220 = bf16[5,1,2048,64]{2,3,1,0:T(8,128)(2,1)} fusion(bf16[5,1,2048,64]{2,3,1,0:T(8,128)(2,1)} %get-tuple-element.438, s32[]{:T(128)S(6)} %copy.60, f32[3,512,2048]{2,1,0:T(8,128)} %fusion.217, f32[3,512,2048]{2,1,0:T(8,128)} %copy-done, f32[3,512]{1,0:T(4,128)S(1)} %dynamic-slice_bitcast_fusion.3, ...), kind=kOutput, calls=%fused_computation.45.clone.1.clone | convolution fusion | flops 437259776 | bytes 53167104 | tf_op jit(solution)/shard_map/while/body/eval_jaxpr/sgqk,sgqd->skd/dot_general | solution.py:208
  413.3 20.1 %fusion.219 = f32[5,1,3,512,64]{3,4,2,1,0:T(8,128)S(1)} fusion(f32[5,1,3,512,64]{3,4,2,1,0:T(8,128)S(1)} %get-tuple-element.437, s32[]{:T(128)S(6)} %copy.60, f32[3,512,2048]{2,1,0:T(8,128)} %fusion.217, f32[3,512,2048]{2,1,0:T(8,128)} %copy-done, f32[3,512]{1,0:T(4,128)S(1)} %dynamic-slice_bitcast_fusion.3, ...), kind=kOutput, calls=%fused_computation.47.clone.1.clone | convolution fusion | flops 437259776 | bytes 53101568 | tf_op jit(solution)/shard_map/while/body/eval_jaxpr/sgqk,skd->sgqd/dot_general | solution.py:205
  442.6 7.4 fusion.217
  450.0 21.2 %fusion.220 = bf16[5,1,2048,64]{2,3,1,0:T(8,128)(2,1)} fusion(bf16[5,1,2048,64]{2,3,1,0:T(8,128)(2,1)} %get-tuple-element.438, s32[]{:T(128)S(6)} %copy.60, f32[3,512,2048]{2,1,0:T(8,128)} %fusion.217, f32[3,512,2048]{2,1,0:T(8,128)} %copy-done, f32[3,512]{1,0:T(4,128)S(1)} %dynamic-slice_bitcast_fusion.3, ...), kind=kOutput, calls=%fused_computation.45.clone.1.clone | convolution fusion | flops 437259776 | bytes 53167104 | tf_op jit(solution)/shard_map/while/body/eval_jaxpr/sgqk,sgqd->skd/dot_general | solution.py:208
  471.2 20.1 %fusion.219 = f32[5,1,3,512,64]{3,4,2,1,0:T(8,128)S(1)} fusion(f32[5,1,3,512,64]{3,4,2,1,0:T(8,128)S(1)} %get-tuple-element.437, s32[]{:T(128)S(6)} %copy.60, f32[3,512,2048]{2,1,0:T(8,128)} %fusion.217, f32[3,512,2048]{2,1,0:T(8,128)} %copy-done, f32[3,512]{1,0:T(4,128)S(1)} %dynamic-slice_bitcast_fusion.3, ...), kind=kOutput, calls=%fused_computation.47.clone.1.clone | convolution fusion | flops 437259776 | bytes 53101568 | tf_op jit(solution)/shard_map/while/body/eval_jaxpr/sgqk,skd->sgqd/dot_general | solution.py:205
  500.5 7.4 fusion.217
  507.9 21.2 %fusion.220 = bf16[5,1,2048,64]{2,3,1,0:T(8,128)(2,1)} fusion(bf16[5,1,2048,64]{2,3,1,0:T(8,128)(2,1)} %get-tuple-element.438, s32[]{:T(128)S(6)} %copy.60, f32[3,512,2048]{2,1,0:T(8,128)} %fusion.217, f32[3,512,2048]{2,1,0:T(8,128)} %copy-done, f32[3,512]{1,0:T(4,128)S(1)} %dynamic-slice_bitcast_fusion.3, ...), kind=kOutput, calls=%fused_computation.45.clone.1.clone | convolution fusion | flops 437259776 | bytes 53167104 | tf_op jit(solution)/shard_map/while/body/eval_jaxpr/sgqk,sgqd->skd/dot_general | solution.py:208
  529.1 20.2 %fusion.219 = f32[5,1,3,512,64]{3,4,2,1,0:T(8,128)S(1)} fusion(f32[5,1,3,512,64]{3,4,2,1,0:T(8,128)S(1)} %get-tuple-element.437, s32[]{:T(128)S(6)} %copy.60, f32[3,512,2048]{2,1,0:T(8,128)} %fusion.217, f32[3,512,2048]{2,1,0:T(8,128)} %copy-done, f32[3,512]{1,0:T(4,128)S(1)} %dynamic-slice_bitcast_fusion.3, ...), kind=kOutput, calls=%fused_computation.47.clone.1.clone | convolution fusion | flops 437259776 | bytes 53101568 | tf_op jit(solution)/shard_map/while/body/eval_jaxpr/sgqk,skd->sgqd/dot_general | solution.py:205
  558.4 7.4 fusion.217
  565.8 21.2 %fusion.220 = bf16[5,1,2048,64]{2,3,1,0:T(8,128)(2,1)} fusion(bf16[5,1,2048,64]{2,3,1,0:T(8,128)(2,1)} %get-tuple-element.438, s32[]{:T(128)S(6)} %copy.60, f32[3,512,2048]{2,1,0:T(8,128)} %fusion.217, f32[3,512,2048]{2,1,0:T(8,128)} %copy-done, f32[3,512]{1,0:T(4,128)S(1)} %dynamic-slice_bitcast_fusion.3, ...), kind=kOutput, calls=%fused_computation.45.clone.1.clone | convolution fusion | flops 437259776 | bytes 53167104 | tf_op jit(solution)/shard_map/while/body/eval_jaxpr/sgqk,sgqd->skd/dot_general | solution.py:208
  587.1 20.1 %fusion.219 = f32[5,1,3,512,64]{3,4,2,1,0:T(8,128)S(1)} fusion(f32[5,1,3,512,64]{3,4,2,1,0:T(8,128)S(1)} %get-tuple-element.437, s32[]{:T(128)S(6)} %copy.60, f32[3,512,2048]{2,1,0:T(8,128)} %fusion.217, f32[3,512,2048]{2,1,0:T(8,128)} %copy-done, f32[3,512]{1,0:T(4,128)S(1)} %dynamic-slice_bitcast_fusion.3, ...), kind=kOutput, calls=%fused_computation.47.clone.1.clone | convolution fusion | flops 437259776 | bytes 53101568 | tf_op jit(solution)/shard_map/while/body/eval_jaxpr/sgqk,skd->sgqd/dot_general | solution.py:205
  616.3 7.4 fusion.217
  623.8 21.2 %fusion.220 = bf16[5,1,2048,64]{2,3,1,0:T(8,128)(2,1)} fusion(bf16[5,1,2048,64]{2,3,1,0:T(8,128)(2,1)} %get-tuple-element.438, s32[]{:T(128)S(6)} %copy.60, f32[3,512,2048]{2,1,0:T(8,128)} %fusion.217, f32[3,512,2048]{2,1,0:T(8,128)} %copy-done, f32[3,512]{1,0:T(4,128)S(1)} %dynamic-slice_bitcast_fusion.3, ...), kind=kOutput, calls=%fused_computation.45.clone.1.clone | convolution fusion | flops 437259776 | bytes 53167104 | tf_op jit(solution)/shard_map/while/body/eval_jaxpr/sgqk,sgqd->skd/dot_general | solution.py:208
  645.0 20.1 %fusion.219 = f32[5,1,3,512,64]{3,4,2,1,0:T(8,128)S(1)} fusion(f32[5,1,3,512,64]{3,4,2,1,0:T(8,128)S(1)} %get-tuple-element.437, s32[]{:T(128)S(6)} %copy.60, f32[3,512,2048]{2,1,0:T(8,128)} %fusion.217, f32[3,512,2048]{2,1,0:T(8,128)} %copy-done, f32[3,512]{1,0:T(4,128)S(1)} %dynamic-slice_bitcast_fusion.3, ...), kind=kOutput, calls=%fused_computation.47.clone.1.clone | convolution fusion | flops 437259776 | bytes 53101568 | tf_op jit(solution)/shard_map/while/body/eval_jaxpr/sgqk,skd->sgqd/dot_general | solution.py:205
  674.9 24.7 %reduce-scatter.12.cloned.1.call-done = bf16[512,320]{0,1:T(8,128)(2,1)} async-done(((bf16[2048,320]{0,1:T(8,128)(2,1)}), bf16[512,320]{0,1:T(8,128)(2,1)}) %reduce-scatter.12.cloned.1.call-update) | async-done | bytes 327696 | tf_op jit(solution)/shard_map/reduce_scatter | solution.py:222
  702.3 30.1 %reduce-scatter.14.cloned.1.call-done = bf16[512,320]{0,1:T(8,128)(2,1)} async-done(((bf16[2048,320]{0,1:T(8,128)(2,1)}), bf16[512,320]{0,1:T(8,128)(2,1)}) %reduce-scatter.14.cloned.1.call-update) | async-done | bytes 327696 | tf_op jit(solution)/shard_map/reduce_scatter | solution.py:228
  734.9 7.0 convolution_convert_fusion
  741.9 7.9 copy.34
  770.4 22.2 %all-reduce.16.cloned.1.call-done = (bf16[960,320]{0,1:T(8,128)(2,1)}, bf16[960,320]{0,1:T(8,128)(2,1)}) async-done(((bf16[960,320]{0,1:T(8,128)(2,1)}, bf16[960,320]{0,1:T(8,128)(2,1)}), (bf16[960,320]{0,1:T(8,128)(2,1)}, bf16[960,320]{0,1:T(8,128)(2,1)})) %all-reduce.16.cloned.1.call-update) | async-done | bytes 1228816
  794.5 62.5 %reduce-scatter.24.cloned.1.call-done = bf16[640,960]{1,0:T(8,128)(2,1)} async-done(((bf16[2560,960]{1,0:T(8,128)(2,1)}), bf16[640,960]{1,0:T(8,128)(2,1)}) %reduce-scatter.24.cloned.1.call-update) | async-done | bytes 1228816
  859.7 35.0 %reduce-scatter.16.cloned.1.call-done = bf16[240,960]{1,0:T(8,128)(2,1)} async-done(((bf16[960,960]{1,0:T(8,128)(2,1)}), bf16[240,960]{1,0:T(8,128)(2,1)}) %reduce-scatter.16.cloned.1.call-update) | async-done | bytes 460816 | tf_op jit(solution)/shard_map/reduce_scatter | solution.py:256
  894.7 37.8 %reduce-scatter.18.cloned.1.call-done = bf16[240,960]{1,0:T(8,128)(2,1)} async-done(((bf16[960,960]{1,0:T(8,128)(2,1)}), bf16[240,960]{1,0:T(8,128)(2,1)}) %reduce-scatter.18.cloned.1.call-update) | async-done | bytes 460816 | tf_op jit(solution)/shard_map/reduce_scatter | solution.py:265
  932.4 61.6 %reduce-scatter.22.cloned.1.call-done = bf16[240,2560]{1,0:T(8,128)(2,1)} async-done(((bf16[960,2560]{1,0:T(8,128)(2,1)}), bf16[240,2560]{1,0:T(8,128)(2,1)}) %reduce-scatter.22.cloned.1.call-update) | async-done | bytes 1228816 | tf_op jit(solution)/shard_map/reduce_scatter | solution.py:271
  994.1 61.6 %reduce-scatter.20.cloned.1.call-done = bf16[240,2560]{1,0:T(8,128)(2,1)} async-done(((bf16[960,2560]{1,0:T(8,128)(2,1)}), bf16[240,2560]{1,0:T(8,128)(2,1)}) %reduce-scatter.20.cloned.1.call-update) | async-done | bytes 1228816 | tf_op jit(solution)/shard_map/reduce_scatter | solution.py:268
  1067.2 9.1 all-reduce.8
  1076.5 15.5 %all-reduce.6 = (bf16[240]{0:T(256)(128)(2,1)S(1)}, bf16[240]{0:T(256)(128)(2,1)S(1)}) all-reduce(bf16[240]{0:T(256)(128)(2,1)S(1)} %dynamic-slice.7, bf16[240]{0:T(256)(128)(2,1)S(1)} %dynamic-slice.9), channel_id=1, replica_groups=mesh['fsdp'=4,'dp'=8] {'dp'}, use_global_device_ids=true, to_apply=%region_29.30 | all-reduce | flops 480 | bytes 1920 | tf_op jit(solution)/shard_map/psum | solution.py:292
  1096.5 77.4 %all-reduce.14.cloned.1.call-done = (bf16[240,960]{1,0:T(8,128)(2,1)}, bf16[240,320]{0,1:T(8,128)(2,1)}, bf16[240,320]{0,1:T(8,128)(2,1)}, bf16[240,960]{1,0:T(8...) async-done(((bf16[240,960]{1,0:T(8,128)(2,1)}, bf16[240,320]{0,1:T(8,128)(2,1)}, bf16[240,320]{0,1:T(8,128)(2,1)}, ...) | async-done | bytes 4915216 | tf_op jit(solution)/shard_map/psum | solution.py:285
  (238 shorter events, 216.8 us)
Async XLA Ops:
  7.2 29.6 %copy-start.3 = (bf16[512,960]{0,1:T(8,128)(2,1)S(1)}, bf16[512,960]{0,1:T(8,128)(2,1)}, u32[]{:S(2)}) copy-start(bf16[512,960]{0,1:T(8,128)(2,1)} %param.16) | copy-start | bytes 2949124
  7.2 28.5 %copy-start.34 = (s32[1,8]{1,0:T(1,128)S(1)}, s32[1,8]{1,0:T(1,128)}, u32[]{:S(2)}) copy-start(s32[1,8]{1,0:T(1,128)} %param.17) | copy-start | bytes 100
  7.2 60.2 %all-gather.12.cloned.1.call-start = ((), (), s32[]{:S(2)}) async-start(), calls=%async_computation.8 | async-start | bytes 1638400 | tf_op jit(solution)/shard_map/all_gather | solution.py:125
  8.8 125.8 %copy-start.30 = (f32[512]{0:T(512)}, f32[512]{0:T(512)S(1)}, u32[]{:S(2)}) copy-start(f32[512]{0:T(512)S(1)} %add_rsqrt_fusion.1) | copy-start | bytes 6148
  23.8 110.7 %copy-start.28 = (f32[960]{0:T(1024)}, f32[960]{0:T(1024)S(1)}, u32[]{:S(2)}) copy-start(f32[960]{0:T(1024)S(1)} %convert_element_type.188) | copy-start | bytes 11524
  35.7 2.6 copy-start.13
  36.8 100.7 %copy-start.16 = (f32[512,32]{0,1:T(8,128)}, f32[512,32]{0,1:T(8,128)S(1)}, u32[]{:S(2)}) copy-start(f32[512,32]{0,1:T(8,128)S(1)} %get-tuple-element.228) | copy-start | bytes 196612
  38.3 60.2 %all-gather.14.cloned.1.call-start = ((), (), s32[]{:S(2)}) async-start(), calls=%async_computation.9 | async-start | bytes 1638400 | tf_op jit(solution)/shard_map/all_gather | solution.py:126
  49.6 3.3 copy-start.11
  50.9 83.7 %all-gather.10.cloned.1.call-start = ((), (), s32[]{:S(2)}) async-start(), calls=%async_computation.7 | async-start | bytes 2457600 | tf_op jit(solution)/shard_map/all_gather | solution.py:81
  51.7 190.5 %all-gather.16.cloned.1.call-start = ((), (), s32[]{:S(2)}) async-start(), calls=%async_computation.10 | async-start | bytes 2457600 | tf_op jit(solution)/shard_map/all_gather | solution.py:84
  52.2 194.7 %all-gather.20.cloned.1.call-start = ((), (), s32[]{:S(2)}) async-start(), calls=%async_computation.12 | async-start | bytes 6144000 | tf_op jit(solution)/shard_map/all_gather | solution.py:86
  52.8 238.6 %all-gather.18.cloned.1.call-start = ((), (), s32[]{:S(2)}) async-start(), calls=%async_computation.11 | async-start | bytes 6144000 | tf_op jit(solution)/shard_map/all_gather | solution.py:85
  53.4 298.6 %all-gather.22.cloned.1.call-start = ((), (), s32[]{:S(2)}) async-start(), calls=%async_computation.13 | async-start | bytes 6144000 | tf_op jit(solution)/shard_map/all_gather | solution.py:87
  54.2 645.4 %reduce-scatter.12.cloned.1.call-start = ((), (), s32[]{:S(2)}) async-start(), calls=%async_computation.14 | async-start | bytes 1638400 | tf_op jit(solution)/shard_map/reduce_scatter | solution.py:222
  246.6 124.7 %copy-start.5 = (f32[512,960]{0,1:T(8,128)}, f32[512,960]{0,1:T(8,128)S(1)}, u32[]{:S(2)}) copy-start(f32[512,960]{0,1:T(8,128)S(1)} %get-tuple-element.232) | copy-start | bytes 5898244
  246.9 44.6 %copy-start.1 = (bf16[512,960]{0,1:T(8,128)(2,1)}, bf16[512,960]{0,1:T(8,128)(2,1)S(1)}, u32[]{:S(2)}) copy-start(bf16[512,960]{0,1:T(8,128)(2,1)S(1)} %multiply_convert_fusion.4) | copy-start | bytes 2949124
  352.0 10.5 copy-start.8
  362.5 2.7 copy-start.36
  362.5 2.7 copy-start.37
  365.2 6.1 copy-start.23
  379.1 5.5 copy-start
  437.0 5.6 copy-start
  494.9 5.5 copy-start
  552.9 5.5 copy-start
  610.8 5.6 copy-start
  670.0 62.4 %reduce-scatter.14.cloned.1.call-start = ((), (), s32[]{:S(2)}) async-start(), calls=%async_computation.15 | async-start | bytes 1638400 | tf_op jit(solution)/shard_map/reduce_scatter | solution.py:228
  673.3 27.3 %copy-start.17 = (f32[512,32]{0,1:T(8,128)S(1)}, f32[512,32]{0,1:T(8,128)}, u32[]{:S(2)}) copy-start(f32[512,32]{0,1:T(8,128)} %copy-done.16) | copy-start | bytes 196612
  673.3 27.3 %copy-start.24 = (f32[512,32]{0,1:T(8,128)S(1)}, f32[512,32]{0,1:T(8,128)}, u32[]{:S(2)}) copy-start(f32[512,32]{0,1:T(8,128)} %get-tuple-element.226) | copy-start | bytes 196612
  674.8 26.0 %copy-start.4 = (bf16[512,960]{0,1:T(8,128)(2,1)S(1)}, bf16[512,960]{0,1:T(8,128)(2,1)}, u32[]{:S(2)}) copy-start(bf16[512,960]{0,1:T(8,128)(2,1)} %param.16) | copy-start | bytes 2949124
  674.8 26.0 %copy-start.29 = (f32[960]{0:T(1024)S(1)}, f32[960]{0:T(1024)}, u32[]{:S(2)}) copy-start(f32[960]{0:T(1024)} %copy-done.28) | copy-start | bytes 11524
  674.8 26.0 %copy-start.31 = (f32[512]{0:T(512)S(1)}, f32[512]{0:T(512)}, u32[]{:S(2)}) copy-start(f32[512]{0:T(512)} %copy-done.30) | copy-start | bytes 6148
  674.8 117.8 %all-reduce.16.cloned.1.call-start = ((), (), s32[]{:S(2)}) async-start(), calls=%async_computation.22 | async-start | bytes 2621440
  700.7 34.1 %copy-start.18 = (bf16[512,5,64]{0,2,1:T(8,128)(2,1)}, bf16[512,5,64]{0,2,1:T(8,128)(2,1)S(1)}, u32[]{:S(2)}) copy-start(bf16[512,5,64]{0,2,1:T(8,128)(2,1)S(1)} %pad_maximum_fusion.2) | copy-start | bytes 983044
  734.9 122.2 %reduce-scatter.24.cloned.1.call-start = ((), (), s32[]{:S(2)}) async-start(), calls=%async_computation.20 | async-start | bytes 6553600
  749.9 144.8 %reduce-scatter.16.cloned.1.call-start = ((), (), s32[]{:S(2)}) async-start(), calls=%async_computation.16 | async-start | bytes 2457600 | tf_op jit(solution)/shard_map/reduce_scatter | solution.py:256
  752.8 4.5 copy-start.2
  752.8 179.6 %reduce-scatter.18.cloned.1.call-start = ((), (), s32[]{:S(2)}) async-start(), calls=%async_computation.17 | async-start | bytes 2457600 | tf_op jit(solution)/shard_map/reduce_scatter | solution.py:265
  757.3 236.7 %reduce-scatter.22.cloned.1.call-start = ((), (), s32[]{:S(2)}) async-start(), calls=%async_computation.19 | async-start | bytes 6144000 | tf_op jit(solution)/shard_map/reduce_scatter | solution.py:271
  763.6 292.1 %reduce-scatter.20.cloned.1.call-start = ((), (), s32[]{:S(2)}) async-start(), calls=%async_computation.18 | async-start | bytes 6144000 | tf_op jit(solution)/shard_map/reduce_scatter | solution.py:268
  769.7 404.2 %all-reduce.14.cloned.1.call-start = ((), (), s32[]{:S(2)}) async-start(), calls=%async_computation.21 | async-start | bytes 9994240 | tf_op jit(solution)/shard_map/psum | solution.py:285
  1055.7 2.9 copy-start.6
  1055.7 2.9 copy-start.35
  1058.6 6.2 copy-start.14
  1058.6 6.2 copy-start.19
  1173.9 5.5 copy-start.25
  1173.9 6.6 copy-start.22
  1179.4 2.8 copy-start.21
  (10 other events, 15.4 us)
Sparse Core Ops, SparseCore 0:
  38.4 28.9 all-gather.11
  69.8 28.6 all-gather.13
  100.3 34.2 all-gather.9
  136.3 34.2 all-gather.15
  172.2 58.6 all-gather.19
  232.7 58.7 all-gather.17
  293.3 58.6 all-gather.21
  670.2 29.3 reduce-scatter.11
  703.0 29.3 reduce-scatter.13
  735.9 56.6 all-reduce.15
  795.6 61.4 reduce-scatter.23
  860.5 34.0 reduce-scatter.15
  898.3 34.0 reduce-scatter.17
  935.3 58.7 reduce-scatter.21
  996.9 58.7 reduce-scatter.19
  1059.1 114.7 all-reduce.13
where the time goes:
time: 1200 us; the launch traced here: 1190 us
  waiting for transfers between devices  570 us (48%)
  matrix products  438 us (36%)
  other arithmetic  63.7 us (5%)
  blocking collectives  56.9 us (5%)
  local copies, waits for them, and re-layouts  45.8 us (4%)
  between operations  16.2 us (1%)
    dot_general x5, matrix products, backward_head(): jnp.einsum('sgqk,sgqd->skd', grad_scores, query, preferred_element_type=j...  106 us
    dot_general x5, matrix products, backward_head(): jnp.einsum('sgqk,skd->sgqd', grad_scores, keys, preferred_element_type=jn...  101 us
    unnamed x18, waiting for transfers between devices  87.8 us
    psum x1, waiting for transfers between devices, on_device(): lax.psum(owned[0].astype(jnp.bfloat16), 'dp').astype(jnp.float32)  77.4 us
    reduce_scatter x1, waiting for transfers between devices, on_device(): lax.psum_scatter(grad_w_up.astype(jnp.bfloat16), 'fsdp', scatter_dimensio...  61.6 us
    reduce_scatter x1, waiting for transfers between devices, on_device(): lax.psum_scatter(grad_w_gate.astype(jnp.bfloat16), 'fsdp', scatter_dimens...  61.6 us
    all_gather x1, waiting for transfers between devices, on_device(): lax.all_gather(w_down, 'fsdp', axis=0, tiled=True)  53.5 us
    reduce_scatter x1, waiting for transfers between devices, on_device(): lax.psum_scatter(grad_w_out.astype(jnp.bfloat16), 'fsdp', scatter_dimensi...  37.8 us
  transfers between devices with their start and end apart: 16, of which 14 were waited for; matrix products, arithmetic and copies ran while one was open for 17% of the time, Pallas kernels for 0%

commit v1 on v0

--- a/solution.py
+++ b/solution.py
@@ -282,7 +282,7 @@
         ).astype(jnp.float32),
     )
     summed = (
-        lax.psum(owned[0].astype(jnp.bfloat16), "dp").astype(jnp.float32),
+        jnp.sum(lax.all_gather(owned[0].astype(jnp.bfloat16), "dp"), axis=0).astype(jnp.float32),
         lax.psum(owned[1].astype(jnp.bfloat16), "dp").astype(jnp.float32),
         lax.psum(owned[2].astype(jnp.bfloat16), "dp").astype(jnp.float32),
         lax.psum(owned[3].astype(jnp.bfloat16), "dp").astype(jnp.float32),

time: 1200 us -> 1270 us (1.058)
  matrix products: 438 us -> 478 us
  waiting for transfers between devices: 570 us -> 601 us
    unnamed x18 -> x19, waiting for transfers between devices: 87.8 us -> 125 us
    all_gather x1, waiting for transfers between devices: 0.02 us -> 36.8 us  [on_device(): lax.all_gather(w_up, 'fsdp', axis=0, tiled=True)]
    all_gather x1, waiting for transfers between devices: 36.7 us -> 0.02 us  [on_device(): lax.all_gather(w_gate, 'fsdp', axis=0, tiled=True)]
    reduce_scatter x1, waiting for transfers between devices: 35 us -> 3.8 us  [on_device(): lax.psum_scatter(grad_w_query.astype(jnp.bfloat16), 'fsdp', scatter_dimen...]
    psum x1, waiting for transfers between devices: 77.4 us -> 103 us  [on_device(): lax.psum(owned[1].astype(jnp.bfloat16), 'dp').astype(jnp.float32)]
    dot_general x5, matrix products: 14.4 us -> 36.9 us  [backward_head(): jnp.einsum('sgqd,skd->sgqk', query, keys, preferred_element_type=jnp.floa...]
    dot_general x5, matrix products: 27.7 us -> 44.2 us  [backward_head(): jnp.einsum('sgqk,sgqd->skd', weights, grad_mixed, preferred_element_type=...]
  transfers between devices with their start and end apart: 16 -> 17, of which waited for: 14 -> 15; matrix products, arithmetic and copies ran while one was open for 17% -> 17% of each run, Pallas kernels for 0% -> 0%
where the time goes in v1:
time: 1270 us
  waiting for transfers between devices  601 us (47%)
  matrix products  478 us (38%)
  other arithmetic  66.7 us (5%)
  blocking collectives  56.9 us (4%)
  local copies, waits for them, and re-layouts  46.7 us (4%)
  between operations  16.3 us (1%)
    unnamed x19, waiting for transfers between devices  125 us
    dot_general x5, matrix products, backward_head(): jnp.einsum('sgqk,sgqd->skd', grad_scores, query, preferred_element_type=j...  106 us
    psum x1, waiting for transfers between devices, on_device(): lax.psum(owned[1].astype(jnp.bfloat16), 'dp').astype(jnp.float32)  103 us
    dot_general x5, matrix products, backward_head(): jnp.einsum('sgqk,skd->sgqd', grad_scores, keys, preferred_element_type=jn...  101 us
    reduce_scatter x1, waiting for transfers between devices, on_device(): lax.psum_scatter(grad_w_gate.astype(jnp.bfloat16), 'fsdp', scatter_dimens...  61.6 us
    reduce_scatter x1, waiting for transfers between devices, on_device(): lax.psum_scatter(grad_w_up.astype(jnp.bfloat16), 'fsdp', scatter_dimensio...  61.6 us
    all_gather x1, waiting for transfers between devices, on_device(): lax.all_gather(w_down, 'fsdp', axis=0, tiled=True)  53.5 us
    dot_general x5, matrix products, backward_head(): jnp.einsum('sgqk,sgqd->skd', weights, grad_mixed, preferred_element_type=...  44.2 us
  transfers between devices with their start and end apart: 17, of which 15 were waited for; matrix products, arithmetic and copies ran while one was open for 17% of the time, Pallas kernels for 0%

profile of v1, /device:TPU:0, one launch (start us, length us, event | category | flops | bytes accessed | tf_op | source)
XLA Modules:
  0.0 1266.9 jit_solution(7804250539364814117)
XLA Ops:
  11.0 11.3 all-reduce.9
  23.9 10.8 all-gather.1
  38.4 10.2 all-gather.2
  55.7 11.7 all-gather.14.cloned.1.call-done
  74.5 23.9 %all-gather.16.cloned.1.call-done = bf16[2048,320]{0,1:T(8,128)(2,1)} async-done(((bf16[512,320]{0,1:T(8,128)(2,1)}), bf16[2048,320]{0,1:T(8,128)(2,1)}) %all-gather.16.cloned.1.call-update) | async-done | bytes 1310736 | tf_op jit(solution)/shard_map/all_gather | solution.py:126
  106.5 28.1 %all-gather.12.cloned.1.call-done = bf16[960,960]{1,0:T(8,128)(2,1)} async-done(((bf16[240,960]{1,0:T(8,128)(2,1)}), bf16[960,960]{1,0:T(8,128)(2,1)}) %all-gather.12.cloned.1.call-update) | async-done | bytes 1843216 | tf_op jit(solution)/shard_map/all_gather | solution.py:81
  137.9 104.1 %while.30 = (s32[]{:T(128)}, bf16[5,1,3,512,64]{3,4,2,1,0:T(8,128)(2,1)}, f32[5,1,3,512,1]{3,2,4,1,0:T(4,128)S(1)}, bf16[5,1,3,512,64]{3,4,2,1,0:T(8,128)(2,1)S(...) while((s32[]{:T(128)}, ...), condition=%wide.region_4.5_spmd.clone.clone, body=%wide.region_1.4_spmd.clone.sunk.clone | while | flops 844102144 | bytes 43124832 | solution.py:147
  246.9 7.8 fusion.126
  254.7 36.8 %all-gather.22.cloned.1.call-done = bf16[960,2560]{1,0:T(8,128)(2,1)} async-done(((bf16[240,2560]{1,0:T(8,128)(2,1)}), bf16[960,2560]{1,0:T(8,128)(2,1)}) %all-gather.22.cloned.1.call-update) | async-done | bytes 4915216 | tf_op jit(solution)/shard_map/all_gather | solution.py:86
  298.5 53.5 %all-gather.24.cloned.1.call-done = bf16[2560,960]{0,1:T(8,128)(2,1)} async-done(((bf16[640,960]{0,1:T(8,128)(2,1)}), bf16[2560,960]{0,1:T(8,128)(2,1)}) %all-gather.24.cloned.1.call-update) | async-done | bytes 4915216 | tf_op jit(solution)/shard_map/all_gather | solution.py:87
  352.0 10.3 multiply_convert_fusion.1
  376.7 329.0 %while.31 = (s32[]{:T(128)}, f32[5,1,3,512,64]{3,4,2,1,0:T(8,128)S(1)}, bf16[5,1,2048,64]{2,3,1,0:T(8,128)(2,1)}, bf16[5,1,2048,64]{2,3,1,0:T(8,128)(2,1)}, bf16...) while((s32[]{:T(128)}, ...), condition=%wide.region_9.10_spmd.clone.clone, body=%wide.region_7.9_spmd.clone.sunk.clone | while | flops 2096110592 | bytes 147784848 | solution.py:213
  376.9 7.4 fusion.217
  384.3 7.4 fusion.218
  392.3 20.2 %fusion.219 = f32[5,1,3,512,64]{3,4,2,1,0:T(8,128)S(1)} fusion(f32[5,1,3,512,64]{3,4,2,1,0:T(8,128)S(1)} %get-tuple-element.436, s32[]{:T(128)S(6)} %copy.60, f32[3,512,2048]{2,1,0:T(8,128)} %fusion.217, f32[3,512,2048]{2,1,0:T(8,128)} %fusion.218, f32[3,512]{1,0:T(4,128)S(1)} %dynamic-slice_bitcast_fusion.3, ...), kind=kOutput, calls=%fused_computation.47.clone.1.clone | convolution fusion | flops 437259776 | bytes 53101568 | tf_op jit(solution)/shard_map/while/body/eval_jaxpr/sgqk,skd->sgqd/dot_general | solution.py:205
  412.5 21.3 %fusion.220 = bf16[5,1,2048,64]{2,3,1,0:T(8,128)(2,1)} fusion(bf16[5,1,2048,64]{2,3,1,0:T(8,128)(2,1)} %get-tuple-element.437, s32[]{:T(128)S(6)} %copy.60, f32[3,512,2048]{2,1,0:T(8,128)} %fusion.217, f32[3,512,2048]{2,1,0:T(8,128)} %fusion.218, f32[3,512]{1,0:T(4,128)S(1)} %dynamic-slice_bitcast_fusion.3, ...), kind=kOutput, calls=%fused_computation.45.clone.1.clone | convolution fusion | flops 437259776 | bytes 53167104 | tf_op jit(solution)/shard_map/while/body/eval_jaxpr/sgqk,sgqd->skd/dot_general | solution.py:208
  433.8 8.8 fusion.221
  442.6 7.4 fusion.217
  450.0 7.4 fusion.218
  458.1 20.1 %fusion.219 = f32[5,1,3,512,64]{3,4,2,1,0:T(8,128)S(1)} fusion(f32[5,1,3,512,64]{3,4,2,1,0:T(8,128)S(1)} %get-tuple-element.436, s32[]{:T(128)S(6)} %copy.60, f32[3,512,2048]{2,1,0:T(8,128)} %fusion.217, f32[3,512,2048]{2,1,0:T(8,128)} %fusion.218, f32[3,512]{1,0:T(4,128)S(1)} %dynamic-slice_bitcast_fusion.3, ...), kind=kOutput, calls=%fused_computation.47.clone.1.clone | convolution fusion | flops 437259776 | bytes 53101568 | tf_op jit(solution)/shard_map/while/body/eval_jaxpr/sgqk,skd->sgqd/dot_general | solution.py:205
  478.2 21.3 %fusion.220 = bf16[5,1,2048,64]{2,3,1,0:T(8,128)(2,1)} fusion(bf16[5,1,2048,64]{2,3,1,0:T(8,128)(2,1)} %get-tuple-element.437, s32[]{:T(128)S(6)} %copy.60, f32[3,512,2048]{2,1,0:T(8,128)} %fusion.217, f32[3,512,2048]{2,1,0:T(8,128)} %fusion.218, f32[3,512]{1,0:T(4,128)S(1)} %dynamic-slice_bitcast_fusion.3, ...), kind=kOutput, calls=%fused_computation.45.clone.1.clone | convolution fusion | flops 437259776 | bytes 53167104 | tf_op jit(solution)/shard_map/while/body/eval_jaxpr/sgqk,sgqd->skd/dot_general | solution.py:208
  499.5 8.8 fusion.221
  508.3 7.4 fusion.217
  515.7 7.4 fusion.218
  523.8 20.2 %fusion.219 = f32[5,1,3,512,64]{3,4,2,1,0:T(8,128)S(1)} fusion(f32[5,1,3,512,64]{3,4,2,1,0:T(8,128)S(1)} %get-tuple-element.436, s32[]{:T(128)S(6)} %copy.60, f32[3,512,2048]{2,1,0:T(8,128)} %fusion.217, f32[3,512,2048]{2,1,0:T(8,128)} %fusion.218, f32[3,512]{1,0:T(4,128)S(1)} %dynamic-slice_bitcast_fusion.3, ...), kind=kOutput, calls=%fused_computation.47.clone.1.clone | convolution fusion | flops 437259776 | bytes 53101568 | tf_op jit(solution)/shard_map/while/body/eval_jaxpr/sgqk,skd->sgqd/dot_general | solution.py:205
  544.0 21.3 %fusion.220 = bf16[5,1,2048,64]{2,3,1,0:T(8,128)(2,1)} fusion(bf16[5,1,2048,64]{2,3,1,0:T(8,128)(2,1)} %get-tuple-element.437, s32[]{:T(128)S(6)} %copy.60, f32[3,512,2048]{2,1,0:T(8,128)} %fusion.217, f32[3,512,2048]{2,1,0:T(8,128)} %fusion.218, f32[3,512]{1,0:T(4,128)S(1)} %dynamic-slice_bitcast_fusion.3, ...), kind=kOutput, calls=%fused_computation.45.clone.1.clone | convolution fusion | flops 437259776 | bytes 53167104 | tf_op jit(solution)/shard_map/while/body/eval_jaxpr/sgqk,sgqd->skd/dot_general | solution.py:208
  565.3 8.8 fusion.221
  574.1 7.4 fusion.217
  581.5 7.4 fusion.218
  589.5 20.1 %fusion.219 = f32[5,1,3,512,64]{3,4,2,1,0:T(8,128)S(1)} fusion(f32[5,1,3,512,64]{3,4,2,1,0:T(8,128)S(1)} %get-tuple-element.436, s32[]{:T(128)S(6)} %copy.60, f32[3,512,2048]{2,1,0:T(8,128)} %fusion.217, f32[3,512,2048]{2,1,0:T(8,128)} %fusion.218, f32[3,512]{1,0:T(4,128)S(1)} %dynamic-slice_bitcast_fusion.3, ...), kind=kOutput, calls=%fused_computation.47.clone.1.clone | convolution fusion | flops 437259776 | bytes 53101568 | tf_op jit(solution)/shard_map/while/body/eval_jaxpr/sgqk,skd->sgqd/dot_general | solution.py:205
  609.7 21.3 %fusion.220 = bf16[5,1,2048,64]{2,3,1,0:T(8,128)(2,1)} fusion(bf16[5,1,2048,64]{2,3,1,0:T(8,128)(2,1)} %get-tuple-element.437, s32[]{:T(128)S(6)} %copy.60, f32[3,512,2048]{2,1,0:T(8,128)} %fusion.217, f32[3,512,2048]{2,1,0:T(8,128)} %fusion.218, f32[3,512]{1,0:T(4,128)S(1)} %dynamic-slice_bitcast_fusion.3, ...), kind=kOutput, calls=%fused_computation.45.clone.1.clone | convolution fusion | flops 437259776 | bytes 53167104 | tf_op jit(solution)/shard_map/while/body/eval_jaxpr/sgqk,sgqd->skd/dot_general | solution.py:208
  630.9 8.8 fusion.221
  639.8 7.4 fusion.217
  647.2 7.4 fusion.218
  655.2 20.2 %fusion.219 = f32[5,1,3,512,64]{3,4,2,1,0:T(8,128)S(1)} fusion(f32[5,1,3,512,64]{3,4,2,1,0:T(8,128)S(1)} %get-tuple-element.436, s32[]{:T(128)S(6)} %copy.60, f32[3,512,2048]{2,1,0:T(8,128)} %fusion.217, f32[3,512,2048]{2,1,0:T(8,128)} %fusion.218, f32[3,512]{1,0:T(4,128)S(1)} %dynamic-slice_bitcast_fusion.3, ...), kind=kOutput, calls=%fused_computation.47.clone.1.clone | convolution fusion | flops 437259776 | bytes 53101568 | tf_op jit(solution)/shard_map/while/body/eval_jaxpr/sgqk,skd->sgqd/dot_general | solution.py:205
  675.4 21.3 %fusion.220 = bf16[5,1,2048,64]{2,3,1,0:T(8,128)(2,1)} fusion(bf16[5,1,2048,64]{2,3,1,0:T(8,128)(2,1)} %get-tuple-element.437, s32[]{:T(128)S(6)} %copy.60, f32[3,512,2048]{2,1,0:T(8,128)} %fusion.217, f32[3,512,2048]{2,1,0:T(8,128)} %fusion.218, f32[3,512]{1,0:T(4,128)S(1)} %dynamic-slice_bitcast_fusion.3, ...), kind=kOutput, calls=%fused_computation.45.clone.1.clone | convolution fusion | flops 437259776 | bytes 53167104 | tf_op jit(solution)/shard_map/while/body/eval_jaxpr/sgqk,sgqd->skd/dot_general | solution.py:208
  696.7 8.8 fusion.221
  719.0 20.9 %reduce-scatter.12.cloned.1.call-done = bf16[512,320]{0,1:T(8,128)(2,1)} async-done(((bf16[2048,320]{0,1:T(8,128)(2,1)}), bf16[512,320]{0,1:T(8,128)(2,1)}) %reduce-scatter.12.cloned.1.call-update) | async-done | bytes 327696 | tf_op jit(solution)/shard_map/reduce_scatter | solution.py:222
  742.5 30.2 %reduce-scatter.14.cloned.1.call-done = bf16[512,320]{0,1:T(8,128)(2,1)} async-done(((bf16[2048,320]{0,1:T(8,128)(2,1)}), bf16[512,320]{0,1:T(8,128)(2,1)}) %reduce-scatter.14.cloned.1.call-update) | async-done | bytes 327696 | tf_op jit(solution)/shard_map/reduce_scatter | solution.py:228
  781.4 7.9 copy.34
  811.1 59.6 %all-reduce.16.cloned.1.call-done = (bf16[960,320]{0,1:T(8,128)(2,1)}, bf16[960,320]{0,1:T(8,128)(2,1)}) async-done(((bf16[960,320]{0,1:T(8,128)(2,1)}, bf16[960,320]{0,1:T(8,128)(2,1)}), (bf16[960,320]{0,1:T(8,128)(2,1)}, bf16[960,320]{0,1:T(8,128)(2,1)})) %all-reduce.16.cloned.1.call-update) | async-done | bytes 1228816
  872.7 62.3 %reduce-scatter.24.cloned.1.call-done = bf16[640,960]{1,0:T(8,128)(2,1)} async-done(((bf16[2560,960]{1,0:T(8,128)(2,1)}), bf16[640,960]{1,0:T(8,128)(2,1)}) %reduce-scatter.24.cloned.1.call-update) | async-done | bytes 1228816
  937.6 35.1 %reduce-scatter.18.cloned.1.call-done = bf16[240,960]{1,0:T(8,128)(2,1)} async-done(((bf16[960,960]{1,0:T(8,128)(2,1)}), bf16[240,960]{1,0:T(8,128)(2,1)}) %reduce-scatter.18.cloned.1.call-update) | async-done | bytes 460816 | tf_op jit(solution)/shard_map/reduce_scatter | solution.py:265
  972.8 61.6 %reduce-scatter.20.cloned.1.call-done = bf16[240,2560]{1,0:T(8,128)(2,1)} async-done(((bf16[960,2560]{1,0:T(8,128)(2,1)}), bf16[240,2560]{1,0:T(8,128)(2,1)}) %reduce-scatter.20.cloned.1.call-update) | async-done | bytes 1228816 | tf_op jit(solution)/shard_map/reduce_scatter | solution.py:268
  1034.4 61.6 %reduce-scatter.22.cloned.1.call-done = bf16[240,2560]{1,0:T(8,128)(2,1)} async-done(((bf16[960,2560]{1,0:T(8,128)(2,1)}), bf16[240,2560]{1,0:T(8,128)(2,1)}) %reduce-scatter.22.cloned.1.call-update) | async-done | bytes 1228816 | tf_op jit(solution)/shard_map/reduce_scatter | solution.py:271
  1107.7 8.9 all-reduce.8
  1116.7 15.8 %all-reduce.6 = (bf16[240]{0:T(256)(128)(2,1)S(1)}, bf16[240]{0:T(256)(128)(2,1)S(1)}) all-reduce(bf16[240]{0:T(256)(128)(2,1)S(1)} %dynamic-slice.7, bf16[240]{0:T(256)(128)(2,1)S(1)} %dynamic-slice.9), channel_id=1, replica_groups=mesh['fsdp'=4,'dp'=8] {'dp'}, use_global_device_ids=true, to_apply=%region_29.30 | all-reduce | flops 480 | bytes 1920 | tf_op jit(solution)/shard_map/psum | solution.py:292
  1146.7 102.6 %all-reduce.14.cloned.1.call-done = (bf16[240,320]{0,1:T(8,128)(2,1)}, bf16[240,320]{0,1:T(8,128)(2,1)}, bf16[240,960]{1,0:T(8,128)(2,1)}, bf16[240,2560]{1,0:T(...) async-done(((bf16[240,320]{0,1:T(8,128)(2,1)}, bf16[240,320]{0,1:T(8,128)(2,1)}, bf16[240,960]{1,0:T(8,128)(2,1)}, bf16[240,2560]{1,0:T(8,128)(2,1)}, ...) | async-done | bytes 4454416 | tf_op jit(solution)/shard_map/psum | solution.py:286
  (228 shorter events, 253.3 us)
Async XLA Ops:
  7.2 29.6 %copy-start.2 = (bf16[512,960]{0,1:T(8,128)(2,1)S(1)}, bf16[512,960]{0,1:T(8,128)(2,1)}, u32[]{:S(2)}) copy-start(bf16[512,960]{0,1:T(8,128)(2,1)} %param.16) | copy-start | bytes 2949124
  7.2 28.5 %copy-start.31 = (s32[1,8]{1,0:T(1,128)S(1)}, s32[1,8]{1,0:T(1,128)}, u32[]{:S(2)}) copy-start(s32[1,8]{1,0:T(1,128)} %param.17) | copy-start | bytes 100
  7.2 60.2 %all-gather.14.cloned.1.call-start = ((), (), s32[]{:S(2)}) async-start(), calls=%async_computation.8 | async-start | bytes 1638400 | tf_op jit(solution)/shard_map/all_gather | solution.py:125
  22.4 112.2 %copy-start.25 = (f32[960]{0:T(1024)}, f32[960]{0:T(1024)S(1)}, u32[]{:S(2)}) copy-start(f32[960]{0:T(1024)S(1)} %convert_element_type.190) | copy-start | bytes 11524
  23.9 110.7 %copy-start.27 = (f32[512]{0:T(512)}, f32[512]{0:T(512)S(1)}, u32[]{:S(2)}) copy-start(f32[512]{0:T(512)S(1)} %add_rsqrt_fusion.1) | copy-start | bytes 6148
  35.7 2.6 copy-start.12
  36.8 100.7 %copy-start.15 = (f32[512,32]{0,1:T(8,128)}, f32[512,32]{0,1:T(8,128)S(1)}, u32[]{:S(2)}) copy-start(f32[512,32]{0,1:T(8,128)S(1)} %get-tuple-element.227) | copy-start | bytes 196612
  36.8 1.5 copy-start.24
  38.3 60.2 %all-gather.16.cloned.1.call-start = ((), (), s32[]{:S(2)}) async-start(), calls=%async_computation.9 | async-start | bytes 1638400 | tf_op jit(solution)/shard_map/all_gather | solution.py:126
  49.6 3.3 copy-start.10
  51.0 83.6 %all-gather.12.cloned.1.call-start = ((), (), s32[]{:S(2)}) async-start(), calls=%async_computation.7 | async-start | bytes 2457600 | tf_op jit(solution)/shard_map/all_gather | solution.py:81
  51.7 190.4 %all-gather.18.cloned.1.call-start = ((), (), s32[]{:S(2)}) async-start(), calls=%async_computation.10 | async-start | bytes 2457600 | tf_op jit(solution)/shard_map/all_gather | solution.py:84
  52.3 194.6 %all-gather.20.cloned.1.call-start = ((), (), s32[]{:S(2)}) async-start(), calls=%async_computation.11 | async-start | bytes 6144000 | tf_op jit(solution)/shard_map/all_gather | solution.py:85
  52.9 238.6 %all-gather.22.cloned.1.call-start = ((), (), s32[]{:S(2)}) async-start(), calls=%async_computation.12 | async-start | bytes 6144000 | tf_op jit(solution)/shard_map/all_gather | solution.py:86
  53.4 298.6 %all-gather.24.cloned.1.call-start = ((), (), s32[]{:S(2)}) async-start(), calls=%async_computation.13 | async-start | bytes 6144000 | tf_op jit(solution)/shard_map/all_gather | solution.py:87
  54.2 685.7 %reduce-scatter.12.cloned.1.call-start = ((), (), s32[]{:S(2)}) async-start(), calls=%async_computation.14 | async-start | bytes 1638400 | tf_op jit(solution)/shard_map/reduce_scatter | solution.py:222
  242.1 1.4 copy-start.9
  246.6 126.1 %copy-start.4 = (f32[512,960]{0,1:T(8,128)}, f32[512,960]{0,1:T(8,128)S(1)}, u32[]{:S(2)}) copy-start(f32[512,960]{0,1:T(8,128)S(1)} %get-tuple-element.231) | copy-start | bytes 5898244
  246.8 44.6 %copy-start = (bf16[512,960]{0,1:T(8,128)(2,1)}, bf16[512,960]{0,1:T(8,128)(2,1)S(1)}, u32[]{:S(2)}) copy-start(bf16[512,960]{0,1:T(8,128)(2,1)S(1)} %multiply_convert_fusion.4) | copy-start | bytes 2949124
  362.3 6.6 copy-start.34
  362.3 6.6 copy-start.33
  362.3 6.6 copy-start.7
  369.0 3.7 copy-start.20
  372.7 1.5 copy-start.30
  374.2 2.1 copy-start.6
  374.2 2.5 copy-start.14
  710.4 62.3 %reduce-scatter.14.cloned.1.call-start = ((), (), s32[]{:S(2)}) async-start(), calls=%async_computation.15 | async-start | bytes 1638400 | tf_op jit(solution)/shard_map/reduce_scatter | solution.py:228
  713.7 1.5 copy-start.16
  713.7 1.5 copy-start.22
  715.2 95.2 %reduce-scatter.16.cloned.1.call-start = ((), (), s32[]{:S(2)}) async-start(), calls=%async_computation.16 | async-start | bytes 2457600 | tf_op jit(solution)/shard_map/reduce_scatter | solution.py:256
  715.2 1.2 copy-start.3
  719.0 151.8 %all-reduce.16.cloned.1.call-start = ((), (), s32[]{:S(2)}) async-start(), calls=%async_computation.23 | async-start | bytes 2621440
  742.5 32.7 %copy-start.21 = (bf16[512,960]{0,1:T(8,128)(2,1)S(1)}, bf16[512,960]{0,1:T(8,128)(2,1)}, u32[]{:S(2)}) copy-start(bf16[512,960]{0,1:T(8,128)(2,1)} %param.27) | copy-start | bytes 2949124
  775.2 159.8 %reduce-scatter.24.cloned.1.call-start = ((), (), s32[]{:S(2)}) async-start(), calls=%async_computation.21 | async-start | bytes 6553600
  789.4 4.7 copy-start.1
  789.4 183.4 %reduce-scatter.18.cloned.1.call-start = ((), (), s32[]{:S(2)}) async-start(), calls=%async_computation.17 | async-start | bytes 2457600 | tf_op jit(solution)/shard_map/reduce_scatter | solution.py:265
  794.0 240.4 %reduce-scatter.20.cloned.1.call-start = ((), (), s32[]{:S(2)}) async-start(), calls=%async_computation.18 | async-start | bytes 6144000 | tf_op jit(solution)/shard_map/reduce_scatter | solution.py:268
  800.2 295.8 %reduce-scatter.22.cloned.1.call-start = ((), (), s32[]{:S(2)}) async-start(), calls=%async_computation.19 | async-start | bytes 6144000 | tf_op jit(solution)/shard_map/reduce_scatter | solution.py:271
  806.5 336.1 %all-gather.26.cloned.1.call-start = ((), (), s32[]{:S(2)}) async-start(), calls=%async_computation.20 | async-start | bytes 4423680 | tf_op jit(solution)/shard_map/all_gather | solution.py:285
  810.4 438.9 %all-reduce.14.cloned.1.call-start = ((), (), s32[]{:S(2)}) async-start(), calls=%async_computation.22 | async-start | bytes 9011200 | tf_op jit(solution)/shard_map/psum | solution.py:286
  1096.1 2.9 copy-start.5
  1096.1 2.9 copy-start.32
  1099.0 6.1 copy-start.13
  1105.1 1.3 copy-start.23
  1106.4 1.2 copy-start.29
  1249.2 5.6 copy-start.19
  1252.7 3.9 copy-start.18
  1256.6 1.7 copy-start.17
  (4 other events, 4.5 us)
Sparse Core Ops, SparseCore 0:
  38.4 28.9 all-gather.13
  69.8 28.6 all-gather.15
  100.3 34.2 all-gather.11
  136.3 34.2 all-gather.17
  172.2 58.7 all-gather.19
  232.7 58.6 all-gather.21
  293.3 58.6 all-gather.23
  710.5 29.3 reduce-scatter.11
  743.4 29.3 reduce-scatter.13
  776.2 34.0 reduce-scatter.15
  814.0 56.6 all-reduce.15
  873.6 61.4 reduce-scatter.23
  938.7 34.0 reduce-scatter.17
  975.7 58.7 reduce-scatter.19
  1037.3 58.7 reduce-scatter.21
  1097.5 45.0 all-gather.25
  1145.9 103.2 all-reduce.13
